TPU v7x, 256 devices: a whole 4x4x8 slice. The times are simulated.
256 devices in a mesh: gx: 16 (over z, x_lo), gy: 8 (over y, core), gz: 2 (over x_hi).
Axes of the slice: x: 4 (x_hi: 2, x_lo: 2; x = x_hi * 2 + x_lo), y: 4, z: 8, core: 2. Of those that a mesh axis runs over, the one named last changes fastest.
Arguments:
- z_factor: float32 [512, 8, 128, 128], P(('gx', 'gy', 'gz')), may hold values from -0.16 to 1.16
- z_columns: int32 [512, 8], replicated, may hold values from 0 to 511, as said below
- p_columns: int32 [512, 8], replicated, may hold values from 0 to 511, as said below
- d_density: float32 [512, 8, 128, 128], P(('gx', 'gy', 'gz')), may hold values from -6 to 6
Outputs:
- adjoint_x: float32 [512, 8, 128, 128], P(('gx', 'gy', 'gz'))
- adjoint_f: float32 [512, 8, 128, 128], P(('gx', 'gy', 'gz'))
Inputs may be any that keep to these rules, and one draw needn't show every extreme that they name: `z_columns`: block row i belongs to atom box i // 2; box b has coordinates (b // 16, (b // 2) % 8, b % 2). Entry [i, 0] is i; the other entries of row i are distinct block rows of the same box or of the boxes next to it by one step along one coordinate, periodically. Exactly one of them lies in i's own box, and at most 2 in any one other box. `p_columns`: same form and same bounds as z_columns.
All inputs are finite; a program needn't handle non-finite values.
Results may differ from a plain program's by a relative error of at most 0.0003.
Values sent between devices are 32-bit elements; how exact they have to be, the bound alone decides.
A program may use at most 128 MiB of HBM per device.

v0:
```python
import jax
import jax.numpy as jnp
from jax import lax
from jax.experimental import pallas as pl
from jax.experimental.pallas import tpu as pltpu
from jax.sharding import PartitionSpec as P

MESH = pl.DeviceIdType.MESH
BLK = 128
WIDE = 256
SLOTS = 8
GX, GY, GZ = 16, 8, 2
ROWS = 512
OWN = 5
NN = (((1,), (0,)), ((), ()))
TN = (((0,), (0,)), ((), ()))
NT = (((1,), (1,)), ((), ()))


def split(x):
    hi = x.astype(jnp.bfloat16)
    return hi, (x - hi.astype(jnp.float32)).astype(jnp.bfloat16)


def product(a, b, dims):
    a_hi, a_lo = split(a)
    b_hi, b_lo = split(b)

    def dot(x, y):
        return lax.dot_general(x, y, dims, preferred_element_type=jnp.float32)

    return dot(a_hi, b_hi) + (dot(a_hi, b_lo) + dot(a_lo, b_hi))


def kernel(
    cols, z_hbm, d_hbm, ox_hbm, of_hbm,
    z_in, d_in, ox, of, zd, dd, zr, zx, yd, yr, yx, ad, ar, an, wd, stz, sty,
    z_at, z_has, p_at, p_has, o_at, n_has,
    local_sem, send_sem, recv_sem,
):
    gx, gy, gz = lax.axis_index("gx"), lax.axis_index("gy"), lax.axis_index("gz")
    sx = 1 - 2 * lax.rem(gx, 2)
    sy = 1 - 2 * lax.rem(gy, 2)
    near = (gx + sx, gy, gz)
    far = (lax.rem(gx - sx + GX, GX), gy, gz)
    over = (gx, gy, 1 - gz)
    core = (gx, gy + sy, gz)
    side = (gx, lax.rem(gy - sy + GY, GY), gz)
    to_z = (lax.rem(gx + 2 * sx + GX, GX), gy, gz)
    from_z = (lax.rem(gx - 2 * sx + GX, GX), gy, gz)
    cross = (gx + sx, gy, 1 - gz)

    def box(where):
        return (where[0] * GY + where[1]) * GZ + where[2]

    boxes = [box(w) for w in (near, far, over, core, side, (gx, gy, gz))]

    load_z = pltpu.make_async_copy(z_hbm, z_in, local_sem.at[0])
    load_d = pltpu.make_async_copy(d_hbm, d_in, local_sem.at[1])
    load_z.start()
    load_d.start()

    barrier = pltpu.get_barrier_semaphore()
    for where in (near, core, side, from_z, cross):
        pl.semaphore_signal(barrier, inc=1, device_id=where, device_id_type=MESH)

    def table(base, at, has):
        for r in range(2):
            row = base + (boxes[OWN] * 2 + r) * SLOTS
            found = [cols[row + s] for s in range(SLOTS)]
            for q in (5, 2, 1, 0, 3, 4):
                for c in range(2):
                    target = boxes[q] * 2 + c
                    slot, hit = jnp.int32(0), jnp.int32(0)
                    for s in range(SLOTS):
                        same = found[s] == target
                        slot = jnp.where(same, s, slot)
                        hit = jnp.where(same, 1, hit)
                    at[r * 12 + q * 2 + c] = slot
                    has[r * 12 + q * 2 + c] = hit

    def spread(blocks, at, has, dense, q):
        for r in range(2):
            for c in range(2):
                i = r * 12 + q * 2 + c
                block = blocks[r * SLOTS + at[i]]
                dense[q, r * BLK : (r + 1) * BLK, c * BLK : (c + 1) * BLK] = jnp.where(has[i] > 0, block, 0.0)

    def keep(x, flags):
        halves = [
            jnp.concatenate([jnp.where(flags[2 * r + c] > 0, x[r * BLK : (r + 1) * BLK, c * BLK : (c + 1) * BLK], 0.0) for c in range(2)], axis=1)
            for r in range(2)
        ]
        return jnp.concatenate(halves, axis=0)

    def own_flags(q):
        return [p_has[r * 12 + q * 2 + c] for r in range(2) for c in range(2)]

    def copy(i, src, dst, where):
        return pltpu.make_async_remote_copy(
            src_ref=src, dst_ref=dst, send_sem=send_sem.at[i], recv_sem=recv_sem.at[i], device_id=where, device_id_type=MESH
        )

    table(0, z_at, z_has)
    load_z.wait()
    spread(z_in, z_at, z_has, zd, OWN)
    pl.semaphore_wait(barrier, 5)

    c = [
        copy(0, zd.at[OWN], zr.at[0], near),
        copy(1, zd.at[2], stz.at[1], near),
        copy(2, zd.at[1], stz.at[0], near),
        copy(3, zd.at[0], zx.at[0], near),
        copy(4, yd.at[2], sty.at[1], near),
        copy(5, yd.at[1], sty.at[0], near),
        copy(6, yd.at[0], yx.at[0], near),
        copy(7, yd.at[OWN], yr.at[0], near),
        copy(8, ad.at[OWN], ar.at[0], near),
    ]
    for q, where in ((3, core), (4, side)):
        i = 9 + 5 * (q - 3)
        c += [
            copy(i, zd.at[OWN], zr.at[q], where),
            copy(i + 1, zd.at[q], zx.at[q], where),
            copy(i + 2, yd.at[q], yx.at[q], where),
            copy(i + 3, yd.at[OWN], yr.at[q], where),
            copy(i + 4, ad.at[OWN], ar.at[q], where),
        ]
    for n, (q, where) in enumerate(((1, to_z), (2, cross))):
        i = 19 + 5 * n
        c += [
            copy(i, zr.at[0], zr.at[q], where),
            copy(i + 1, stz.at[n], zx.at[q], where),
            copy(i + 2, sty.at[n], yx.at[q], where),
            copy(i + 3, yr.at[0], yr.at[q], where),
            copy(i + 4, ar.at[0], ar.at[q], where),
        ]
    NEAR, CORE, SIDE, FAR, OVER = 0, 9, 14, 19, 24

    c[CORE].start()
    c[SIDE].start()
    c[0].start()
    for q, i in ((2, 1), (1, 2), (0, 3), (3, CORE + 1), (4, SIDE + 1)):
        spread(z_in, z_at, z_has, zd, q)
        c[i].start()

    table(ROWS * SLOTS, p_at, p_has)
    for r in range(2):
        row = ROWS * SLOTS + (boxes[OWN] * 2 + r) * SLOTS
        for s in range(SLOTS):
            column = cols[row + s]
            place = jnp.int32(0)
            for q in range(6):
                for k in range(2):
                    place = jnp.where(column == boxes[q] * 2 + k, q * 2 + k, place)
            o_at[r * SLOTS + s] = place
    for q in range(5):
        for r in range(2):
            row = ROWS * SLOTS + (boxes[q] * 2 + r) * SLOTS
            found = [cols[row + s] for s in range(SLOTS)]
            for k in range(2):
                hit = jnp.int32(0)
                for s in range(SLOTS):
                    hit = jnp.where(found[s] == boxes[OWN] * 2 + k, 1, hit)
                n_has[q * 4 + r * 2 + k] = hit
    load_d.wait()
    for q in (5, 3, 4, 0, 2, 1):
        spread(d_in, p_at, p_has, dd, q)

    @pl.loop(0, 6)
    def _(q):
        yd[q] = product(dd[OWN], zd[q], NN)

    def finish_y(q):
        yd[q] = keep(yd[q] + product(dd[q], zr[q], NN), own_flags(q))

    def gather_y(q):
        yd[OWN] += product(dd[q], zx[q], NN)

    c[CORE].wait_recv()
    finish_y(3)
    c[CORE + 2].start()
    c[SIDE].wait_recv()
    finish_y(4)
    c[SIDE + 2].start()
    c[0].wait_recv()
    c[FAR].start()
    c[OVER].start()
    finish_y(0)
    c[CORE + 1].wait_recv()
    gather_y(3)
    c[SIDE + 1].wait_recv()
    gather_y(4)
    c[1].wait_recv()
    c[OVER + 1].start()
    c[OVER].wait_recv()
    finish_y(2)
    c[4].start()
    c[FAR].wait_recv()
    finish_y(1)
    c[5].start()
    c[6].start()
    c[2].wait_recv()
    c[FAR + 1].start()
    c[OVER + 1].wait_recv()
    gather_y(2)
    c[3].wait_recv()
    gather_y(0)
    c[FAR + 1].wait_recv()
    gather_y(1)
    c[7].start()
    c[CORE + 3].start()
    c[SIDE + 3].start()

    @pl.loop(0, 6)
    def _(q):
        ad[q] = product(zd[OWN], yd[q], TN)

    def gather_a(q):
        ad[OWN] += product(zx[q], yx[q], TN)

    c[CORE + 2].wait_recv()
    gather_a(3)
    c[SIDE + 2].wait_recv()
    gather_a(4)
    c[4].wait_recv()
    c[OVER + 2].start()
    c[5].wait_recv()
    c[FAR + 2].start()
    c[6].wait_recv()
    gather_a(0)
    c[OVER + 2].wait_recv()
    gather_a(2)
    c[FAR + 2].wait_recv()
    gather_a(1)
    c[8].start()
    c[CORE + 4].start()
    c[SIDE + 4].start()

    c[7].wait_recv()
    c[FAR + 3].start()
    c[OVER + 3].start()

    @pl.loop(0, 5)
    def _(q):
        x = product(zr[q], yx[q], TN) + product(zd[q], yd[OWN], TN)
        an[q] = keep(x, [n_has[q * 4 + k] for k in range(4)])

    wd[OWN] = product(zd[OWN], ad[OWN], NN)

    @pl.loop(0, 5)
    def _(q):
        wd[OWN] += product(zd[q], an[q], NN)

    c[CORE + 3].wait_recv()
    c[SIDE + 3].wait_recv()
    c[FAR + 3].wait_recv()
    c[OVER + 3].wait_recv()

    @pl.loop(0, 5)
    def _(q):
        ad[q] = keep(ad[q] + product(zx[q], yr[q], TN), own_flags(q))
        wd[q] = product(zd[OWN], ad[q], NN)

    def collect(dense, out):
        for r in range(2):
            for s in range(SLOTS):
                place = o_at[r * SLOTS + s]
                both = dense[lax.div(place, 2), r * BLK : (r + 1) * BLK]
                out[r * SLOTS + s] = jnp.where(lax.rem(place, 2) > 0, both[:, BLK:], both[:, :BLK])

    collect(ad, ox)
    store_x = pltpu.make_async_copy(ox, ox_hbm, local_sem.at[2])
    store_x.start()

    c[8].wait_recv()
    c[FAR + 4].start()
    c[OVER + 4].start()
    yf = wd
    c[CORE + 4].wait_recv()
    c[SIDE + 4].wait_recv()
    c[FAR + 4].wait_recv()
    c[OVER + 4].wait_recv()

    an[0] = product(wd[OWN], zd[OWN], NT)

    @pl.loop(0, 5)
    def _(q):
        w = keep(wd[q] + product(zd[q], ar[q], NN), own_flags(q))
        an[0] += product(w, zd[q], NT)
        yf[q] = product(wd[OWN], zx[q], NT) + product(w, zr[q], NT)

    wd[OWN] = an[0]
    collect(wd, of)
    store_f = pltpu.make_async_copy(of, of_hbm, local_sem.at[3])
    store_f.start()
    for one in c:
        one.wait_send()
    store_x.wait()
    store_f.wait()


def shards(z_factor, z_columns, p_columns, d_density):
    cols = jnp.concatenate([z_columns.reshape(-1), p_columns.reshape(-1)])
    tiles = (2 * SLOTS, BLK, BLK)
    wide = (WIDE, WIDE)
    f32 = jnp.float32
    counts = [6, 6, 5, 5, 6, 5, 5, 6, 5, 5, 6, 2, 2]
    out_x, out_f = pl.pallas_call(
        kernel,
        out_shape=[jax.ShapeDtypeStruct(tiles, f32)] * 2,
        in_specs=[pl.BlockSpec(memory_space=pltpu.SMEM)] + [pl.BlockSpec(memory_space=pl.ANY)] * 2,
        out_specs=[pl.BlockSpec(memory_space=pl.ANY)] * 2,
        scratch_shapes=[pltpu.VMEM(tiles, f32)] * 4
        + [pltpu.VMEM((n,) + wide, f32) for n in counts]
        + [pltpu.SMEM((n,), jnp.int32) for n in (24, 24, 24, 24, 16, 20)]
        + [pltpu.SemaphoreType.DMA((4,)), pltpu.SemaphoreType.DMA((29,)), pltpu.SemaphoreType.DMA((29,))],
        compiler_params=pltpu.CompilerParams(collective_id=0, has_side_effects=True, vmem_limit_bytes=48 * 1024 * 1024),
    )(cols, z_factor.reshape(tiles), d_density.reshape(tiles))
    shape = z_factor.shape
    return out_x.reshape(shape), out_f.reshape(shape)


def solution(mesh):
    spec = P(("gx", "gy", "gz"), None, None, None)
    return jax.shard_map(shards, mesh=mesh, in_specs=(spec, P(), P(), spec), out_specs=(spec, spec), check_vma=False)
```

profile of v0, /device:TPU:8, one launch (start us, length us, event | category | flops | bytes accessed | tf_op | source)
XLA Modules:
  0.0 84.2 jit_solution(15745877989358688759)
XLA Ops:
  0.6 0.0 copy-start
  0.6 0.9 %copy.6 = s32[512,8]{1,0:T(8,128)S(1)} copy(s32[512,8]{0,1:T(8,128)} %param.5) | data formatting | bytes 32768 | tf_op args[1]
  1.6 0.1 reshape.22
  1.7 0.8 copy.7
  2.6 0.1 reshape.23
  2.7 0.0 copy-done
  2.8 0.0 copy-start.1
  2.8 1.2 %copy-done.1 = f32[2,8,128,128]{3,2,1,0:T(8,128)S(1)} copy-done((f32[2,8,128,128]{3,2,1,0:T(8,128)S(1)}, f32[2,8,128,128]{3,2,1,0:T(8,128)}, u32[]{:S(2)}) %copy-start.1) | copy-done | bytes 1048600
  4.0 78.3 %shard_map.59 = (f32[16,128,128]{2,1,0:T(8,128)S(1)}, f32[16,128,128]{2,1,0:T(8,128)S(1)}) custom-call(s32[8192]{0:T(1024)S(1)} %pad_add_fusion.cols, f32[16,128,128]{2,1,0:T(8,128)S(1)} %bitcast.4, f32[16,128,128]{2,1,0:T(8,128)S(1)} %bitcast.5), custom_call_target="tpu_custom_call" | custom-call | tf_op jit(solution)/shard_map/pallas_call | solution.py:309
  82.3 1.0 %copy.10 = f32[2,8,128,128]{3,2,1,0:T(8,128)} copy(f32[2,8,128,128]{3,2,1,0:T(8,128)S(1)} %bitcast.7) | data formatting | bytes 2097152
  83.2 1.0 %copy.11 = f32[2,8,128,128]{3,2,1,0:T(8,128)} copy(f32[2,8,128,128]{3,2,1,0:T(8,128)S(1)} %bitcast.6) | data formatting | bytes 2097152
  (1 shorter events, 0.0 us)
Async XLA Ops:
  0.6 2.1 %copy-start = (f32[2,8,128,128]{3,2,1,0:T(8,128)S(1)}, f32[2,8,128,128]{3,2,1,0:T(8,128)}, u32[]{:S(2)}) copy-start(f32[2,8,128,128]{3,2,1,0:T(8,128)} %param.4) | copy-start | bytes 3145732
  2.8 1.2 %copy-start.1 = (f32[2,8,128,128]{3,2,1,0:T(8,128)S(1)}, f32[2,8,128,128]{3,2,1,0:T(8,128)}, u32[]{:S(2)}) copy-start(f32[2,8,128,128]{3,2,1,0:T(8,128)} %param.7) | copy-start | bytes 3145732
where the time goes:
time: 84.4 us; the launch traced here: 84.2 us
  Pallas kernels  78.3 us (93%)
  local copies, waits for them, and re-layouts  5.23 us (6%)
    pallas_call x1, Pallas kernels, shards(): pl.pallas_call(kernel, out_shape=[jax.ShapeDtypeStruct(tiles, f32)] * 2,...  78.3 us
    unnamed x8, local copies, waits for them, and re-layouts  4.93 us

commit v1 on v0

v1 whole, which is shorter than its diff:
```python
import jax
import jax.numpy as jnp
from jax import lax
from jax.experimental import pallas as pl
from jax.experimental.pallas import tpu as pltpu
from jax.sharding import PartitionSpec as P

MESH = pl.DeviceIdType.MESH
BLK = 128
WIDE = 256
SLOTS = 8
GX, GY, GZ = 16, 8, 2
ROWS = 512
OWN = 5
NN = (((1,), (0,)), ((), ()))
TN = (((0,), (0,)), ((), ()))
NT = (((1,), (1,)), ((), ()))


def split(x):
    hi = x.astype(jnp.bfloat16)
    return hi, (x - hi.astype(jnp.float32)).astype(jnp.bfloat16)


def product(a, b, dims):
    a_hi, a_lo = split(a)
    b_hi, b_lo = split(b)

    def dot(x, y):
        return lax.dot_general(x, y, dims, preferred_element_type=jnp.float32)

    return dot(a_hi, b_hi) + (dot(a_hi, b_lo) + dot(a_lo, b_hi))


def kernel(
    zc_hbm, pc_hbm, z_hbm, d_hbm, ox_hbm, of_hbm,
    z_in, d_in, ox, of, zd, dd, zr, zx, yd, yr, yx, ad, ar, an, wd, fd,
    z_cols, p_cols, z_at, z_has, p_at, p_has, o_at, n_has,
    local_sem, send_sem, recv_sem,
):
    gx, gy, gz = lax.axis_index("gx"), lax.axis_index("gy"), lax.axis_index("gz")
    sx = 1 - 2 * lax.rem(gx, 2)
    sy = 1 - 2 * lax.rem(gy, 2)
    near = (gx + sx, gy, gz)
    far = (lax.rem(gx - sx + GX, GX), gy, gz)
    over = (gx, gy, 1 - gz)
    core = (gx, gy + sy, gz)
    side = (gx, lax.rem(gy - sy + GY, GY), gz)
    to_z = (lax.rem(gx + 2 * sx + GX, GX), gy, gz)
    from_z = (lax.rem(gx - 2 * sx + GX, GX), gy, gz)
    cross = (gx + sx, gy, 1 - gz)

    def box(where):
        return (where[0] * GY + where[1]) * GZ + where[2]

    boxes = [box(w) for w in (near, far, over, core, side, (gx, gy, gz))]

    load_z = pltpu.make_async_copy(z_hbm, z_in, local_sem.at[0])
    load_d = pltpu.make_async_copy(d_hbm, d_in, local_sem.at[1])
    load_zc = pltpu.make_async_copy(zc_hbm, z_cols, local_sem.at[4])
    load_pc = pltpu.make_async_copy(pc_hbm, p_cols, local_sem.at[5])
    load_zc.start()
    load_z.start()
    load_pc.start()
    load_d.start()

    barrier = pltpu.get_barrier_semaphore()
    for where in (near, far, over, core, side, from_z, cross):
        pl.semaphore_signal(barrier, inc=1, device_id=where, device_id_type=MESH)

    def table(cols, at, has):
        for r in range(2):
            row = boxes[OWN] * 2 + r
            found = [cols[s, row] for s in range(SLOTS)]
            for q in (5, 2, 1, 0, 3, 4):
                for c in range(2):
                    target = boxes[q] * 2 + c
                    slot, hit = jnp.int32(0), jnp.int32(0)
                    for s in range(SLOTS):
                        same = found[s] == target
                        slot = jnp.where(same, s, slot)
                        hit = jnp.where(same, 1, hit)
                    at[r * 12 + q * 2 + c] = slot
                    has[r * 12 + q * 2 + c] = hit

    def spread(blocks, at, has, dense, q):
        for r in range(2):
            for c in range(2):
                i = r * 12 + q * 2 + c
                block = blocks[r * SLOTS + at[i]]
                dense[q, r * BLK : (r + 1) * BLK, c * BLK : (c + 1) * BLK] = jnp.where(has[i] > 0, block, 0.0)

    def keep(x, flags):
        halves = [
            jnp.concatenate([jnp.where(flags[2 * r + c] > 0, x[r * BLK : (r + 1) * BLK, c * BLK : (c + 1) * BLK], 0.0) for c in range(2)], axis=1)
            for r in range(2)
        ]
        return jnp.concatenate(halves, axis=0)

    def own_flags(q):
        return [p_has[r * 12 + q * 2 + c] for r in range(2) for c in range(2)]

    def copy(i, src, dst, where):
        return pltpu.make_async_remote_copy(
            src_ref=src, dst_ref=dst, send_sem=send_sem.at[i], recv_sem=recv_sem.at[i], device_id=where, device_id_type=MESH
        )

    load_zc.wait()
    table(z_cols, z_at, z_has)
    load_z.wait()
    spread(z_in, z_at, z_has, zd, OWN)
    pl.semaphore_wait(barrier, 7)

    c = {}

    def message(name, src, dst, where):
        c[name] = copy(len(c), src, dst, where)

    half = [pl.ds(0, BLK), pl.ds(BLK, BLK)]
    message("z0", zd.at[OWN], zr.at[0], near)
    for q, where in ((3, core), (4, side)):
        message(f"z{q}", zd.at[OWN], zr.at[q], where)
        message(f"y{q}", yd.at[OWN], yr.at[q], where)
        message(f"a{q}", ad.at[OWN], ar.at[q], where)
    for q, where in enumerate((near, far, over, core, side)):
        message(f"zx{q}", zd.at[q], zx.at[q], where)
        message(f"yx{q}", yd.at[q], yx.at[q], where)
    for h in range(2):
        message(f"y0{h}", yd.at[OWN, half[h]], yr.at[0, half[h]], near)
        message(f"a0{h}", ad.at[OWN, half[h]], ar.at[0, half[h]], near)
    for q, where in ((1, to_z), (2, cross)):
        message(f"z{q}", zr.at[0], zr.at[q], where)
        for h in range(2):
            message(f"y{q}{h}", yr.at[0, half[h]], yr.at[q, half[h]], where)
            message(f"a{q}{h}", ar.at[0, half[h]], ar.at[q, half[h]], where)

    def send(*names):
        for name in names:
            c[name].start()

    def arrive(*names):
        for name in names:
            c[name].wait_recv()

    def tables():
        table(p_cols, p_at, p_has)
        for r in range(2):
            row = boxes[OWN] * 2 + r
            for s in range(SLOTS):
                column = p_cols[s, row]
                place = jnp.int32(0)
                for q in range(6):
                    for k in range(2):
                        place = jnp.where(column == boxes[q] * 2 + k, q * 2 + k, place)
                o_at[r * SLOTS + s] = place
        for q in range(5):
            for r in range(2):
                row = boxes[q] * 2 + r
                found = [p_cols[s, row] for s in range(SLOTS)]
                for k in range(2):
                    hit = jnp.int32(0)
                    for s in range(SLOTS):
                        hit = jnp.where(found[s] == boxes[OWN] * 2 + k, 1, hit)
                    n_has[q * 4 + r * 2 + k] = hit

    send("z0", "z3", "z4")
    for q in (2, 1, 0, 3, 4):
        spread(z_in, z_at, z_has, zd, q)
        send(f"zx{q}")

    load_pc.wait()
    tables()
    load_d.wait()
    for q in (5, 3, 4, 0, 2, 1):
        spread(d_in, p_at, p_has, dd, q)

    @pl.loop(0, 6)
    def _(q):
        yd[q] = product(dd[OWN], zd[q], NN)

    def finish_y(q):
        yd[q] = keep(yd[q] + product(dd[q], zr[q], NN), own_flags(q))

    def gather_y(q):
        yd[OWN] += product(dd[q], zx[q], NN)

    arrive("z3")
    finish_y(3)
    send("yx3")
    arrive("z4")
    finish_y(4)
    send("yx4")
    arrive("z0")
    send("z1", "z2")
    finish_y(0)
    arrive("zx3")
    gather_y(3)
    arrive("zx4")
    gather_y(4)
    arrive("z2")
    finish_y(2)
    send("yx2")
    arrive("z1")
    finish_y(1)
    send("yx1", "yx0")
    arrive("zx2")
    gather_y(2)

    @pl.loop(0, 5)
    def _(q):
        ad[q] = product(zd[OWN], yd[q], TN)

    arrive("zx1")
    gather_y(1)
    arrive("zx0")
    gather_y(0)
    send("y00", "y01", "y3", "y4")

    ad[OWN] = product(zd[OWN], yd[OWN], TN)

    @pl.loop(0, 5)
    def _(q):
        an[q] = product(zd[q], yd[OWN], TN)

    def gather_a(q):
        ad[OWN] += product(zx[q], yx[q], TN)

    def other_a(q):
        an[q] = keep(an[q] + product(zr[q], yx[q], TN), [n_has[q * 4 + k] for k in range(4)])

    def finish_a(q):
        ad[q] = keep(ad[q] + product(zx[q], yr[q], TN), own_flags(q))
        wd[q] = product(zd[OWN], ad[q], NN)

    for q in (3, 4):
        arrive(f"yx{q}")
        gather_a(q)
        other_a(q)
    for q in (3, 4):
        arrive(f"y{q}")
        finish_a(q)
    for q in (2, 1):
        arrive(f"yx{q}")
        gather_a(q)
        other_a(q)
    arrive("yx0")
    gather_a(0)
    send("a00", "a01", "a3", "a4")
    other_a(0)
    arrive("y00")
    send("y10", "y20")

    wd[OWN] = product(zd[OWN], ad[OWN], NN)

    @pl.loop(0, 5)
    def _(q):
        wd[OWN] += product(zd[q], an[q], NN)

    arrive("y01")
    send("y11", "y21")
    finish_a(0)

    @pl.loop(0, 5)
    def _(q):
        fd[q] = product(wd[OWN], zx[q], NT)

    fd[OWN] = product(wd[OWN], zd[OWN], NT)
    arrive("a00")
    send("a10", "a20")
    arrive("y10", "y11")
    finish_a(1)
    arrive("y20", "y21")
    finish_a(2)

    def collect(dense, out):
        for r in range(2):
            for s in range(SLOTS):
                place = o_at[r * SLOTS + s]
                both = dense[lax.div(place, 2), r * BLK : (r + 1) * BLK]
                out[r * SLOTS + s] = jnp.where(lax.rem(place, 2) > 0, both[:, BLK:], both[:, :BLK])

    def finish_f(q):
        w = keep(wd[q] + product(zd[q], ar[q], NN), own_flags(q))
        fd[OWN] += product(w, zd[q], NT)
        fd[q] += product(w, zr[q], NT)

    arrive("a01")
    send("a11", "a21")
    collect(ad, ox)
    store_x = pltpu.make_async_copy(ox, ox_hbm, local_sem.at[2])
    store_x.start()
    arrive("a3")
    finish_f(3)
    arrive("a4")
    finish_f(4)
    finish_f(0)
    arrive("a10", "a11")
    finish_f(1)
    arrive("a20", "a21")
    finish_f(2)
    collect(fd, of)
    store_f = pltpu.make_async_copy(of, of_hbm, local_sem.at[3])
    store_f.start()
    for one in c.values():
        one.wait_send()
    store_x.wait()
    store_f.wait()


def shards(z_factor, z_columns, p_columns, d_density):
    tiles = (2 * SLOTS, BLK, BLK)
    wide = (WIDE, WIDE)
    f32 = jnp.float32
    counts = [6, 6, 5, 5, 6, 5, 5, 6, 5, 5, 6, 6]
    out_x, out_f = pl.pallas_call(
        kernel,
        out_shape=[jax.ShapeDtypeStruct(tiles, f32)] * 2,
        in_specs=[pl.BlockSpec(memory_space=pltpu.HBM)] * 4,
        out_specs=[pl.BlockSpec(memory_space=pl.ANY)] * 2,
        scratch_shapes=[pltpu.VMEM(tiles, f32)] * 4
        + [pltpu.VMEM((n,) + wide, f32) for n in counts]
        + [pltpu.SMEM((SLOTS, ROWS), jnp.int32)] * 2
        + [pltpu.SMEM((n,), jnp.int32) for n in (24, 24, 24, 24, 16, 20)]
        + [pltpu.SemaphoreType.DMA((6,)), pltpu.SemaphoreType.DMA((31,)), pltpu.SemaphoreType.DMA((31,))],
        compiler_params=pltpu.CompilerParams(collective_id=0, has_side_effects=True, vmem_limit_bytes=48 * 1024 * 1024),
    )(*(pltpu.with_memory_space_constraint(x, pltpu.HBM) for x in (z_columns.T, p_columns.T, z_factor.reshape(tiles), d_density.reshape(tiles))))
    shape = z_factor.shape
    return out_x.reshape(shape), out_f.reshape(shape)


def solution(mesh):
    spec = P(("gx", "gy", "gz"), None, None, None)
    return jax.shard_map(shards, mesh=mesh, in_specs=(spec, P(), P(), spec), out_specs=(spec, spec), check_vma=False)
```

time: 84.4 us -> 72.6 us (0.86)
  the two profiles are of different devices: /device:TPU:8 before, /device:TPU:1 now
where the time goes in v1:
time: 72.6 us; the launch traced here: 72.1 us
  Pallas kernels  69.6 us (96%)
  local copies, waits for them, and re-layouts  1.94 us (3%)
    pallas_call x1, Pallas kernels, shards(): pl.pallas_call(kernel, out_shape=[jax.ShapeDtypeStruct(tiles, f32)] * 2,...  69.6 us
    unnamed x2, local copies, waits for them, and re-layouts  1.94 us

profile of v1, /device:TPU:1, one launch (start us, length us, event | category | flops | bytes accessed | tf_op | source)
XLA Modules:
  0.0 72.1 jit_solution(17707726931659468773)
XLA Ops:
  0.6 69.6 %shard_map.59 = (f32[16,128,128]{2,1,0:T(8,128)S(1)}, f32[16,128,128]{2,1,0:T(8,128)S(1)}) custom-call(s32[8,512]{1,0:T(8,128)} %bitcast.10, s32[8,512]{1,0:T(8,128)} %bitcast.11, f32[16,128,128]{2,1,0:T(8,128)} %bitcast.8, f32[16,128,128]{2,1,0:T(8,128)} %bitcast.9), custom_call_target="tpu_custom_call" | custom-call | tf_op jit(solution)/shard_map/pallas_call | solution.py:315
  70.2 1.0 %copy.8 = f32[2,8,128,128]{3,2,1,0:T(8,128)} copy(f32[2,8,128,128]{3,2,1,0:T(8,128)S(1)} %bitcast.7) | data formatting | bytes 2097152
  71.2 1.0 %copy.9 = f32[2,8,128,128]{3,2,1,0:T(8,128)} copy(f32[2,8,128,128]{3,2,1,0:T(8,128)S(1)} %bitcast.6) | data formatting | bytes 2097152

commit v2 on v1

--- a/solution.py
+++ b/solution.py
@@ -34,7 +34,7 @@
 
 def kernel(
     zc_hbm, pc_hbm, z_hbm, d_hbm, ox_hbm, of_hbm,
-    z_in, d_in, ox, of, zd, dd, zr, zx, yd, yr, yx, ad, ar, an, wd, fd,
+    z_in, d_in, ox, of, zd, dd, zr, zx, yd, yr, yx, ad, ar, an, wd, fd, pd, pr, sr, rd, rr, via, qd, ur,
     z_cols, p_cols, z_at, z_has, p_at, p_has, o_at, n_has,
     local_sem, send_sem, recv_sem,
 ):
@@ -65,7 +65,7 @@
     load_d.start()
 
     barrier = pltpu.get_barrier_semaphore()
-    for where in (near, far, over, core, side, from_z, cross):
+    for where in (near, far, over, core, side, from_z, to_z, cross):
         pl.semaphore_signal(barrier, inc=1, device_id=where, device_id_type=MESH)
 
     def table(cols, at, has):
@@ -109,7 +109,7 @@
     table(z_cols, z_at, z_has)
     load_z.wait()
     spread(z_in, z_at, z_has, zd, OWN)
-    pl.semaphore_wait(barrier, 7)
+    pl.semaphore_wait(barrier, 8)
 
     c = {}
 
@@ -120,17 +120,23 @@
     message("z0", zd.at[OWN], zr.at[0], near)
     for q, where in ((3, core), (4, side)):
         message(f"z{q}", zd.at[OWN], zr.at[q], where)
+        message(f"zx{q}", zd.at[q], zx.at[q], where)
         message(f"y{q}", yd.at[OWN], yr.at[q], where)
         message(f"a{q}", ad.at[OWN], ar.at[q], where)
-    for q, where in enumerate((near, far, over, core, side)):
-        message(f"zx{q}", zd.at[q], zx.at[q], where)
-        message(f"yx{q}", yd.at[q], yx.at[q], where)
+        message(f"yx{q}", yd.at[q], yx.at[q - 3], where)
+    message("zx0", zd.at[0], zx.at[0], near)
+    message("s", pd.at[0], sr, near)
+    message("u", qd, ur, near)
+    for q, where, back in ((1, to_z, from_z), (2, cross, cross)):
+        message(f"z{q}", zr.at[0], zr.at[q], where)
+        message(f"via{q}", zd.at[q], via.at[q - 1], near)
+        message(f"zx{q}", via.at[q - 1], zx.at[q], where)
+        message(f"p{q}", pd.at[q], pr.at[q - 1], back)
+        message(f"r{q}", rd.at[q], rr.at[q - 1], back)
     for h in range(2):
         message(f"y0{h}", yd.at[OWN, half[h]], yr.at[0, half[h]], near)
         message(f"a0{h}", ad.at[OWN, half[h]], ar.at[0, half[h]], near)
-    for q, where in ((1, to_z), (2, cross)):
-        message(f"z{q}", zr.at[0], zr.at[q], where)
-        for h in range(2):
+        for q, where in ((1, to_z), (2, cross)):
             message(f"y{q}{h}", yr.at[0, half[h]], yr.at[q, half[h]], where)
             message(f"a{q}{h}", ar.at[0, half[h]], ar.at[q, half[h]], where)
 
@@ -153,20 +159,20 @@
                     for k in range(2):
                         place = jnp.where(column == boxes[q] * 2 + k, q * 2 + k, place)
                 o_at[r * SLOTS + s] = place
-        for q in range(5):
+        own, near_box = boxes[OWN], boxes[0]
+        for q, rows, columns in ((0, box(to_z), near_box), (1, box(cross), near_box), (3, boxes[3], own), (4, boxes[4], own)):
             for r in range(2):
-                row = boxes[q] * 2 + r
-                found = [p_cols[s, row] for s in range(SLOTS)]
+                found = [p_cols[s, rows * 2 + r] for s in range(SLOTS)]
                 for k in range(2):
                     hit = jnp.int32(0)
                     for s in range(SLOTS):
-                        hit = jnp.where(found[s] == boxes[OWN] * 2 + k, 1, hit)
+                        hit = jnp.where(found[s] == columns * 2 + k, 1, hit)
                     n_has[q * 4 + r * 2 + k] = hit
 
     send("z0", "z3", "z4")
-    for q in (2, 1, 0, 3, 4):
+    for q, name in ((3, "zx3"), (4, "zx4"), (1, "via1"), (2, "via2"), (0, "zx0")):
         spread(z_in, z_at, z_has, zd, q)
-        send(f"zx{q}")
+        send(name)
 
     load_pc.wait()
     tables()
@@ -190,87 +196,98 @@
     arrive("z4")
     finish_y(4)
     send("yx4")
+    def offer(q):
+        pd[q] = product(zd[q], yd[q], TN)
+
     arrive("z0")
     send("z1", "z2")
     finish_y(0)
+    offer(0)
     arrive("zx3")
     gather_y(3)
     arrive("zx4")
     gather_y(4)
+    arrive("via1")
+    send("zx1")
+    arrive("z1")
+    finish_y(1)
+    offer(1)
+    send("p1")
     arrive("z2")
     finish_y(2)
-    send("yx2")
-    arrive("z1")
-    finish_y(1)
-    send("yx1", "yx0")
+    offer(2)
+    send("p2")
+
+    @pl.loop(0, 5)
+    def _(q):
+        rd[q] = product(zd[OWN], yd[q], TN)
+
+    send("r1")
+    arrive("via2")
+    send("zx2", "r2")
+    arrive("zx1")
+    gather_y(1)
+    arrive("p1", "p2")
+    pd[0] += pr[0] + pr[1]
+    send("s")
+    arrive("zx0")
+    gather_y(0)
     arrive("zx2")
     gather_y(2)
-
-    @pl.loop(0, 5)
-    def _(q):
-        ad[q] = product(zd[OWN], yd[q], TN)
-
-    arrive("zx1")
-    gather_y(1)
-    arrive("zx0")
-    gather_y(0)
     send("y00", "y01", "y3", "y4")
 
     ad[OWN] = product(zd[OWN], yd[OWN], TN)
-
-    @pl.loop(0, 5)
-    def _(q):
-        an[q] = product(zd[q], yd[OWN], TN)
-
-    def gather_a(q):
-        ad[OWN] += product(zx[q], yx[q], TN)
-
-    def other_a(q):
-        an[q] = keep(an[q] + product(zr[q], yx[q], TN), [n_has[q * 4 + k] for k in range(4)])
-
-    def finish_a(q):
-        ad[q] = keep(ad[q] + product(zx[q], yr[q], TN), own_flags(q))
-        wd[q] = product(zd[OWN], ad[q], NN)
-
     for q in (3, 4):
         arrive(f"yx{q}")
-        gather_a(q)
-        other_a(q)
+        ad[OWN] += product(zx[q], yx[q - 3], TN)
+        x = product(zr[q], yx[q - 3], TN) + product(zd[q], yd[OWN], TN)
+        an[q - 3] = keep(x, [n_has[q * 4 + k] for k in range(4)])
+    arrive("s")
+    ad[OWN] += sr[...]
+    send("a00", "a01", "a3", "a4")
+
+    def finish_a(q):
+        ad[q] = keep(rd[q] + product(zx[q], yr[q], TN), own_flags(q))
+
+    def finish_w(q):
+        wd[q] = product(zd[OWN], ad[q], NN)
+
     for q in (3, 4):
         arrive(f"y{q}")
         finish_a(q)
-    for q in (2, 1):
-        arrive(f"yx{q}")
-        gather_a(q)
-        other_a(q)
-    arrive("yx0")
-    gather_a(0)
-    send("a00", "a01", "a3", "a4")
-    other_a(0)
-    arrive("y00")
-    send("y10", "y20")
-
-    wd[OWN] = product(zd[OWN], ad[OWN], NN)
-
-    @pl.loop(0, 5)
-    def _(q):
-        wd[OWN] += product(zd[q], an[q], NN)
-
-    arrive("y01")
-    send("y11", "y21")
+        finish_w(q)
+    wd[OWN] = product(zd[OWN], ad[OWN], NN) + (product(zd[3], an[0], NN) + product(zd[4], an[1], NN))
+    arrive("r1", "r2")
+    for h in range(2):
+        arrive(f"y0{h}")
+        send(f"y1{h}", f"y2{h}")
     finish_a(0)
-
-    @pl.loop(0, 5)
-    def _(q):
-        fd[q] = product(wd[OWN], zx[q], NT)
-
-    fd[OWN] = product(wd[OWN], zd[OWN], NT)
+    qd[...] = product(zx[0], ad[0], NN)
+    for k in range(2):
+        x = keep(rr[k] + product(via[k], yr[0], TN), [n_has[k * 4 + i] for i in range(4)])
+        qd[...] += product(via[k], x, NN)
+    send("u")
+    fd[OWN] = jnp.zeros((WIDE, WIDE), jnp.float32)
+
+    def start_f(q):
+        w = keep(wd[q] + product(zd[q], ar[q], NN), own_flags(q))
+        fd[OWN] += product(w, zd[q], NT)
+        fd[q] = product(w, zr[q], NT)
+
+    arrive("a3")
+    start_f(3)
     arrive("a00")
     send("a10", "a20")
-    arrive("y10", "y11")
-    finish_a(1)
-    arrive("y20", "y21")
-    finish_a(2)
+    arrive("a4")
+    start_f(4)
+    for q in (1, 2):
+        arrive(f"y{q}0", f"y{q}1")
+        finish_a(q)
+    arrive("a01")
+    send("a11", "a21")
+    for q in (0, 1, 2):
+        finish_w(q)
+    start_f(0)
 
     def collect(dense, out):
         for r in range(2):
@@ -279,25 +296,20 @@
                 both = dense[lax.div(place, 2), r * BLK : (r + 1) * BLK]
                 out[r * SLOTS + s] = jnp.where(lax.rem(place, 2) > 0, both[:, BLK:], both[:, :BLK])
 
-    def finish_f(q):
-        w = keep(wd[q] + product(zd[q], ar[q], NN), own_flags(q))
-        fd[OWN] += product(w, zd[q], NT)
-        fd[q] += product(w, zr[q], NT)
-
-    arrive("a01")
-    send("a11", "a21")
     collect(ad, ox)
     store_x = pltpu.make_async_copy(ox, ox_hbm, local_sem.at[2])
     store_x.start()
-    arrive("a3")
-    finish_f(3)
-    arrive("a4")
-    finish_f(4)
-    finish_f(0)
-    arrive("a10", "a11")
-    finish_f(1)
-    arrive("a20", "a21")
-    finish_f(2)
+    for q in (1, 2):
+        arrive(f"a{q}0", f"a{q}1")
+        start_f(q)
+    arrive("u")
+    wd[OWN] += ur[...]
+
+    @pl.loop(0, 5)
+    def _(q):
+        fd[q] += product(wd[OWN], zx[q], NT)
+
+    fd[OWN] += product(wd[OWN], zd[OWN], NT)
     collect(fd, of)
     store_f = pltpu.make_async_copy(of, of_hbm, local_sem.at[3])
     store_f.start()
@@ -311,17 +323,17 @@
     tiles = (2 * SLOTS, BLK, BLK)
     wide = (WIDE, WIDE)
     f32 = jnp.float32
-    counts = [6, 6, 5, 5, 6, 5, 5, 6, 5, 5, 6, 6]
+    counts = [6, 6, 5, 5, 6, 5, 2, 6, 5, 2, 6, 6, 3, 2, 0, 5, 2, 2, 0, 0]
     out_x, out_f = pl.pallas_call(
         kernel,
         out_shape=[jax.ShapeDtypeStruct(tiles, f32)] * 2,
         in_specs=[pl.BlockSpec(memory_space=pltpu.HBM)] * 4,
         out_specs=[pl.BlockSpec(memory_space=pl.ANY)] * 2,
         scratch_shapes=[pltpu.VMEM(tiles, f32)] * 4
-        + [pltpu.VMEM((n,) + wide, f32) for n in counts]
+        + [pltpu.VMEM((n,) + wide if n else wide, f32) for n in counts]
         + [pltpu.SMEM((SLOTS, ROWS), jnp.int32)] * 2
         + [pltpu.SMEM((n,), jnp.int32) for n in (24, 24, 24, 24, 16, 20)]
-        + [pltpu.SemaphoreType.DMA((6,)), pltpu.SemaphoreType.DMA((31,)), pltpu.SemaphoreType.DMA((31,))],
+        + [pltpu.SemaphoreType.DMA((36,)), pltpu.SemaphoreType.DMA((36,)), pltpu.SemaphoreType.DMA((37,))],
         compiler_params=pltpu.CompilerParams(collective_id=0, has_side_effects=True, vmem_limit_bytes=48 * 1024 * 1024),
     )(*(pltpu.with_memory_space_constraint(x, pltpu.HBM) for x in (z_columns.T, p_columns.T, z_factor.reshape(tiles), d_density.reshape(tiles))))
     shape = z_factor.shape

time: 72.6 us -> 65.7 us (0.905)
  Pallas kernels: 69.6 us -> 62.9 us
    pallas_call x1, Pallas kernels: 69.6 us -> 62.9 us  [shards(): pl.pallas_call(kernel, out_shape=[jax.ShapeDtypeStruct(tiles, f32)] * 2,...]
where the time goes in v2:
time: 65.7 us; the launch traced here: 65.5 us
  Pallas kernels  62.9 us (96%)
  local copies, waits for them, and re-layouts  1.94 us (3%)
    pallas_call x1, Pallas kernels, shards(): pl.pallas_call(kernel, out_shape=[jax.ShapeDtypeStruct(tiles, f32)] * 2,...  62.9 us
    unnamed x2, local copies, waits for them, and re-layouts  1.94 us

profile of v2, /device:TPU:1, one launch (start us, length us, event | category | flops | bytes accessed | tf_op | source)
XLA Modules:
  0.0 65.5 jit_solution(3632690470146220142)
XLA Ops:
  0.6 62.9 %shard_map.59 = (f32[16,128,128]{2,1,0:T(8,128)S(1)}, f32[16,128,128]{2,1,0:T(8,128)S(1)}) custom-call(s32[8,512]{1,0:T(8,128)} %bitcast.10, s32[8,512]{1,0:T(8,128)} %bitcast.11, f32[16,128,128]{2,1,0:T(8,128)} %bitcast.8, f32[16,128,128]{2,1,0:T(8,128)} %bitcast.9), custom_call_target="tpu_custom_call" | custom-call | tf_op jit(solution)/shard_map/pallas_call | solution.py:327
  63.6 1.0 %copy.8 = f32[2,8,128,128]{3,2,1,0:T(8,128)} copy(f32[2,8,128,128]{3,2,1,0:T(8,128)S(1)} %bitcast.7) | data formatting | bytes 2097152
  64.5 1.0 %copy.9 = f32[2,8,128,128]{3,2,1,0:T(8,128)} copy(f32[2,8,128,128]{3,2,1,0:T(8,128)S(1)} %bitcast.6) | data formatting | bytes 2097152

commit v3 on v2

--- a/solution.py
+++ b/solution.py
@@ -11,6 +11,7 @@
 SLOTS = 8
 GX, GY, GZ = 16, 8, 2
 ROWS = 512
+CUT_Z, CUT_V, CUT = 1, 1, 4
 OWN = 5
 NN = (((1,), (0,)), ((), ()))
 TN = (((0,), (0,)), ((), ()))
@@ -23,8 +24,8 @@
 
 
 def product(a, b, dims):
-    a_hi, a_lo = split(a)
-    b_hi, b_lo = split(b)
+    a_hi, a_lo = a if isinstance(a, tuple) else split(a)
+    b_hi, b_lo = b if isinstance(b, tuple) else split(b)
 
     def dot(x, y):
         return lax.dot_general(x, y, dims, preferred_element_type=jnp.float32)
@@ -35,6 +36,7 @@
 def kernel(
     zc_hbm, pc_hbm, z_hbm, d_hbm, ox_hbm, of_hbm,
     z_in, d_in, ox, of, zd, dd, zr, zx, yd, yr, yx, ad, ar, an, wd, fd, pd, pr, sr, rd, rr, via, qd, ur,
+    zd_hi, zd_lo, zx_hi, zx_lo, w_hi, w_lo,
     z_cols, p_cols, z_at, z_has, p_at, p_has, o_at, n_has,
     local_sem, send_sem, recv_sem,
 ):
@@ -116,8 +118,13 @@
     def message(name, src, dst, where):
         c[name] = copy(len(c), src, dst, where)
 
-    half = [pl.ds(0, BLK), pl.ds(BLK, BLK)]
-    message("z0", zd.at[OWN], zr.at[0], near)
+    def parts(name, count, src, dst, where):
+        rows = WIDE // count
+        for h in range(count):
+            part = pl.ds(h * rows, rows)
+            message(f"{name}{h}", src.at[part], dst.at[part], where)
+
+    parts("z0", CUT_Z, zd.at[OWN], zr.at[0], near)
     for q, where in ((3, core), (4, side)):
         message(f"z{q}", zd.at[OWN], zr.at[q], where)
         message(f"zx{q}", zd.at[q], zx.at[q], where)
@@ -127,18 +134,16 @@
     message("zx0", zd.at[0], zx.at[0], near)
     message("s", pd.at[0], sr, near)
     message("u", qd, ur, near)
+    parts("y0", CUT, yd.at[OWN], yr.at[0], near)
+    parts("a0", CUT, ad.at[OWN], ar.at[0], near)
     for q, where, back in ((1, to_z, from_z), (2, cross, cross)):
-        message(f"z{q}", zr.at[0], zr.at[q], where)
-        message(f"via{q}", zd.at[q], via.at[q - 1], near)
-        message(f"zx{q}", via.at[q - 1], zx.at[q], where)
+        parts(f"z{q}", CUT_Z, zr.at[0], zr.at[q], where)
+        parts(f"via{q}", CUT_V, zd.at[q], via.at[q - 1], near)
+        parts(f"zx{q}", CUT_V, via.at[q - 1], zx.at[q], where)
         message(f"p{q}", pd.at[q], pr.at[q - 1], back)
         message(f"r{q}", rd.at[q], rr.at[q - 1], back)
-    for h in range(2):
-        message(f"y0{h}", yd.at[OWN, half[h]], yr.at[0, half[h]], near)
-        message(f"a0{h}", ad.at[OWN, half[h]], ar.at[0, half[h]], near)
-        for q, where in ((1, to_z), (2, cross)):
-            message(f"y{q}{h}", yr.at[0, half[h]], yr.at[q, half[h]], where)
-            message(f"a{q}{h}", ar.at[0, half[h]], ar.at[q, half[h]], where)
+        parts(f"y{q}", CUT, yr.at[0], yr.at[q], where)
+        parts(f"a{q}", CUT, ar.at[0], ar.at[q], where)
 
     def send(*names):
         for name in names:
@@ -147,6 +152,14 @@
     def arrive(*names):
         for name in names:
             c[name].wait_recv()
+
+    def all_of(name, count):
+        return [f"{name}{h}" for h in range(count)]
+
+    def relay(name, count, *onward):
+        for h in range(count):
+            arrive(f"{name}{h}")
+            send(*(f"{other}{h}" for other in onward))
 
     def tables():
         table(p_cols, p_at, p_has)
@@ -169,10 +182,10 @@
                         hit = jnp.where(found[s] == columns * 2 + k, 1, hit)
                     n_has[q * 4 + r * 2 + k] = hit
 
-    send("z0", "z3", "z4")
+    send("z3", "z4", *all_of("z0", CUT_Z))
     for q, name in ((3, "zx3"), (4, "zx4"), (1, "via1"), (2, "via2"), (0, "zx0")):
         spread(z_in, z_at, z_has, zd, q)
-        send(name)
+        send(*(all_of(name, CUT_V) if q in (1, 2) else [name]))
 
     load_pc.wait()
     tables()
@@ -180,15 +193,23 @@
     for q in (5, 3, 4, 0, 2, 1):
         spread(d_in, p_at, p_has, dd, q)
 
+    def own_z(q):
+        return zd_hi[q], zd_lo[q]
+
+    def near_z(q):
+        return zx_hi[q], zx_lo[q]
+
     @pl.loop(0, 6)
     def _(q):
-        yd[q] = product(dd[OWN], zd[q], NN)
+        zd_hi[q], zd_lo[q] = split(zd[q])
+        yd[q] = product(dd[OWN], own_z(q), NN)
 
     def finish_y(q):
         yd[q] = keep(yd[q] + product(dd[q], zr[q], NN), own_flags(q))
 
     def gather_y(q):
-        yd[OWN] += product(dd[q], zx[q], NN)
+        zx_hi[q], zx_lo[q] = split(zx[q])
+        yd[OWN] += product(dd[q], near_z(q), NN)
 
     arrive("z3")
     finish_y(3)
@@ -197,94 +218,90 @@
     finish_y(4)
     send("yx4")
     def offer(q):
-        pd[q] = product(zd[q], yd[q], TN)
-
-    arrive("z0")
-    send("z1", "z2")
+        pd[q] = product(own_z(q), yd[q], TN)
+
+    relay("z0", CUT_Z, "z1", "z2")
     finish_y(0)
     offer(0)
     arrive("zx3")
     gather_y(3)
     arrive("zx4")
     gather_y(4)
-    arrive("via1")
-    send("zx1")
-    arrive("z1")
+    relay("via1", CUT_V, "zx1")
+    arrive(*all_of("z1", CUT_Z))
     finish_y(1)
     offer(1)
     send("p1")
-    arrive("z2")
+    arrive(*all_of("z2", CUT_Z))
     finish_y(2)
     offer(2)
     send("p2")
 
     @pl.loop(0, 5)
     def _(q):
-        rd[q] = product(zd[OWN], yd[q], TN)
+        rd[q] = product(own_z(OWN), yd[q], TN)
 
     send("r1")
-    arrive("via2")
-    send("zx2", "r2")
-    arrive("zx1")
+    relay("via2", CUT_V, "zx2")
+    send("r2")
+    arrive(*all_of("zx1", CUT_V))
     gather_y(1)
     arrive("p1", "p2")
     pd[0] += pr[0] + pr[1]
     send("s")
     arrive("zx0")
     gather_y(0)
-    arrive("zx2")
+    arrive(*all_of("zx2", CUT_V))
     gather_y(2)
-    send("y00", "y01", "y3", "y4")
-
-    ad[OWN] = product(zd[OWN], yd[OWN], TN)
+    send(*all_of("y0", CUT), "y3", "y4")
+
+    ad[OWN] = product(own_z(OWN), yd[OWN], TN)
     for q in (3, 4):
         arrive(f"yx{q}")
-        ad[OWN] += product(zx[q], yx[q - 3], TN)
-        x = product(zr[q], yx[q - 3], TN) + product(zd[q], yd[OWN], TN)
+        ad[OWN] += product(near_z(q), yx[q - 3], TN)
+        x = product(zr[q], yx[q - 3], TN) + product(own_z(q), yd[OWN], TN)
         an[q - 3] = keep(x, [n_has[q * 4 + k] for k in range(4)])
     arrive("s")
     ad[OWN] += sr[...]
-    send("a00", "a01", "a3", "a4")
+    send(*all_of("a0", CUT), "a3", "a4")
 
     def finish_a(q):
-        ad[q] = keep(rd[q] + product(zx[q], yr[q], TN), own_flags(q))
+        ad[q] = keep(rd[q] + product(near_z(q), yr[q], TN), own_flags(q))
 
     def finish_w(q):
-        wd[q] = product(zd[OWN], ad[q], NN)
+        wd[q] = product(own_z(OWN), ad[q], NN)
 
     for q in (3, 4):
         arrive(f"y{q}")
         finish_a(q)
         finish_w(q)
-    wd[OWN] = product(zd[OWN], ad[OWN], NN) + (product(zd[3], an[0], NN) + product(zd[4], an[1], NN))
+    wd[OWN] = product(own_z(OWN), ad[OWN], NN) + (product(zd[3], an[0], NN) + product(zd[4], an[1], NN))
     arrive("r1", "r2")
-    for h in range(2):
-        arrive(f"y0{h}")
-        send(f"y1{h}", f"y2{h}")
-    finish_a(0)
-    qd[...] = product(zx[0], ad[0], NN)
-    for k in range(2):
-        x = keep(rr[k] + product(via[k], yr[0], TN), [n_has[k * 4 + i] for i in range(4)])
-        qd[...] += product(via[k], x, NN)
+    relay("y0", CUT, "y1", "y2")
+    hop = [split(via[k]) for k in range(2)]
+    y_near = split(yr[0])
+    raw = [product(near_z(0), y_near, TN)] + [product(hop[k], y_near, TN) for k in range(2)]
+    x0 = keep(rd[0] + raw[0], own_flags(0))
+    x1, x2 = (keep(rr[k] + raw[k + 1], [n_has[k * 4 + i] for i in range(4)]) for k in range(2))
+    qd[...] = product(near_z(0), x0, NN) + product(hop[0], x1, NN) + product(hop[1], x2, NN)
     send("u")
+    ad[0] = x0
     fd[OWN] = jnp.zeros((WIDE, WIDE), jnp.float32)
 
-    def start_f(q):
-        w = keep(wd[q] + product(zd[q], ar[q], NN), own_flags(q))
-        fd[OWN] += product(w, zd[q], NT)
-        fd[q] = product(w, zr[q], NT)
-
-    arrive("a3")
-    start_f(3)
-    arrive("a00")
-    send("a10", "a20")
-    arrive("a4")
-    start_f(4)
+    def start_f(*qs):
+        raw = [product(own_z(q), ar[q], NN) for q in qs]
+        ws = [split(keep(wd[q] + x, own_flags(q))) for q, x in zip(qs, raw)]
+        for q, w in zip(qs, ws):
+            fd[q] = product(w, zr[q], NT)
+        own = [product(w, own_z(q), NT) for q, w in zip(qs, ws)]
+        fd[OWN] += own[0] if len(qs) == 1 else own[0] + own[1]
+
+    relay("a0", CUT, "a1", "a2")
+    arrive("a3", "a4")
+    start_f(3, 4)
     for q in (1, 2):
-        arrive(f"y{q}0", f"y{q}1")
+        arrive(*all_of(f"y{q}", CUT))
         finish_a(q)
-    arrive("a01")
-    send("a11", "a21")
     for q in (0, 1, 2):
         finish_w(q)
     start_f(0)
@@ -299,17 +316,16 @@
     collect(ad, ox)
     store_x = pltpu.make_async_copy(ox, ox_hbm, local_sem.at[2])
     store_x.start()
-    for q in (1, 2):
-        arrive(f"a{q}0", f"a{q}1")
-        start_f(q)
+    arrive(*all_of("a1", CUT), *all_of("a2", CUT))
+    start_f(1, 2)
     arrive("u")
-    wd[OWN] += ur[...]
-
-    @pl.loop(0, 5)
+    w_hi[...], w_lo[...] = split(wd[OWN] + ur[...])
+
+    @pl.loop(0, 5, unroll=5)
     def _(q):
-        fd[q] += product(wd[OWN], zx[q], NT)
-
-    fd[OWN] += product(wd[OWN], zd[OWN], NT)
+        fd[q] += product((w_hi[...], w_lo[...]), near_z(q), NT)
+
+    fd[OWN] += product((w_hi[...], w_lo[...]), own_z(OWN), NT)
     collect(fd, of)
     store_f = pltpu.make_async_copy(of, of_hbm, local_sem.at[3])
     store_f.start()
@@ -331,9 +347,10 @@
         out_specs=[pl.BlockSpec(memory_space=pl.ANY)] * 2,
         scratch_shapes=[pltpu.VMEM(tiles, f32)] * 4
         + [pltpu.VMEM((n,) + wide if n else wide, f32) for n in counts]
+        + [pltpu.VMEM((n,) + wide if n else wide, jnp.bfloat16) for n in (6, 6, 5, 5, 0, 0)]
         + [pltpu.SMEM((SLOTS, ROWS), jnp.int32)] * 2
         + [pltpu.SMEM((n,), jnp.int32) for n in (24, 24, 24, 24, 16, 20)]
-        + [pltpu.SemaphoreType.DMA((36,)), pltpu.SemaphoreType.DMA((36,)), pltpu.SemaphoreType.DMA((37,))],
+        + [pltpu.SemaphoreType.DMA((6,)), pltpu.SemaphoreType.DMA((48,)), pltpu.SemaphoreType.DMA((48,))],
         compiler_params=pltpu.CompilerParams(collective_id=0, has_side_effects=True, vmem_limit_bytes=48 * 1024 * 1024),
     )(*(pltpu.with_memory_space_constraint(x, pltpu.HBM) for x in (z_columns.T, p_columns.T, z_factor.reshape(tiles), d_density.reshape(tiles))))
     shape = z_factor.shape

time: 65.7 us -> 63.1 us (0.960)
  Pallas kernels: 62.9 us -> 60.4 us
    pallas_call x1, Pallas kernels: 62.9 us -> 60.4 us  [shards(): pl.pallas_call(kernel, out_shape=[jax.ShapeDtypeStruct(tiles, f32)] * 2,...]
where the time goes in v3:
time: 63.1 us; the launch traced here: 63 us
  Pallas kernels  60.4 us (96%)
  local copies, waits for them, and re-layouts  1.94 us (3%)
  between operations  0.64 us (1%)
    pallas_call x1, Pallas kernels, shards(): pl.pallas_call(kernel, out_shape=[jax.ShapeDtypeStruct(tiles, f32)] * 2,...  60.4 us
    unnamed x2, local copies, waits for them, and re-layouts  1.94 us

profile of v3, /device:TPU:1, one launch (start us, length us, event | category | flops | bytes accessed | tf_op | source)
XLA Modules:
  0.0 63.0 jit_solution(14194709566552898975)
XLA Ops:
  0.6 60.4 %shard_map.59 = (f32[16,128,128]{2,1,0:T(8,128)S(1)}, f32[16,128,128]{2,1,0:T(8,128)S(1)}) custom-call(s32[8,512]{1,0:T(8,128)} %bitcast.10, s32[8,512]{1,0:T(8,128)} %bitcast.11, f32[16,128,128]{2,1,0:T(8,128)} %bitcast.8, f32[16,128,128]{2,1,0:T(8,128)} %bitcast.9), custom_call_target="tpu_custom_call" | custom-call | tf_op jit(solution)/shard_map/pallas_call | solution.py:343
  61.0 1.0 %copy.8 = f32[2,8,128,128]{3,2,1,0:T(8,128)} copy(f32[2,8,128,128]{3,2,1,0:T(8,128)S(1)} %bitcast.7) | data formatting | bytes 2097152
  62.0 1.0 %copy.9 = f32[2,8,128,128]{3,2,1,0:T(8,128)} copy(f32[2,8,128,128]{3,2,1,0:T(8,128)S(1)} %bitcast.6) | data formatting | bytes 2097152

commit v4 on v3

--- a/solution.py
+++ b/solution.py
@@ -34,8 +34,8 @@
 
 
 def kernel(
-    zc_hbm, pc_hbm, z_hbm, d_hbm, ox_hbm, of_hbm,
-    z_in, d_in, ox, of, zd, dd, zr, zx, yd, yr, yx, ad, ar, an, wd, fd, pd, pr, sr, rd, rr, via, qd, ur,
+    zc_hbm, pc_hbm, z_hbm, d_hbm, ox, of,
+    z_in, d_in, zd, dd, zr, zx, yd, yr, yx, ad, ar, an, wd, fd, pd, pr, sr, rd, rr, via, qd, ur,
     zd_hi, zd_lo, zx_hi, zx_lo, w_hi, w_lo,
     z_cols, p_cols, z_at, z_has, p_at, p_has, o_at, n_has,
     local_sem, send_sem, recv_sem,
@@ -314,8 +314,6 @@
                 out[r * SLOTS + s] = jnp.where(lax.rem(place, 2) > 0, both[:, BLK:], both[:, :BLK])
 
     collect(ad, ox)
-    store_x = pltpu.make_async_copy(ox, ox_hbm, local_sem.at[2])
-    store_x.start()
     arrive(*all_of("a1", CUT), *all_of("a2", CUT))
     start_f(1, 2)
     arrive("u")
@@ -327,12 +325,16 @@
 
     fd[OWN] += product((w_hi[...], w_lo[...]), own_z(OWN), NT)
     collect(fd, of)
-    store_f = pltpu.make_async_copy(of, of_hbm, local_sem.at[3])
-    store_f.start()
     for one in c.values():
         one.wait_send()
-    store_x.wait()
-    store_f.wait()
+
+
+def deliver(x, f, out_x, out_f, sem):
+    copies = [pltpu.make_async_copy(x, out_x, sem.at[0]), pltpu.make_async_copy(f, out_f, sem.at[1])]
+    for one in copies:
+        one.start()
+    for one in copies:
+        one.wait()
 
 
 def shards(z_factor, z_columns, p_columns, d_density):
@@ -342,10 +344,10 @@
     counts = [6, 6, 5, 5, 6, 5, 2, 6, 5, 2, 6, 6, 3, 2, 0, 5, 2, 2, 0, 0]
     out_x, out_f = pl.pallas_call(
         kernel,
-        out_shape=[jax.ShapeDtypeStruct(tiles, f32)] * 2,
+        out_shape=[pltpu.VMEM(tiles, f32)] * 2,
         in_specs=[pl.BlockSpec(memory_space=pltpu.HBM)] * 4,
-        out_specs=[pl.BlockSpec(memory_space=pl.ANY)] * 2,
-        scratch_shapes=[pltpu.VMEM(tiles, f32)] * 4
+        out_specs=[pl.BlockSpec(memory_space=pltpu.VMEM)] * 2,
+        scratch_shapes=[pltpu.VMEM(tiles, f32)] * 2
         + [pltpu.VMEM((n,) + wide if n else wide, f32) for n in counts]
         + [pltpu.VMEM((n,) + wide if n else wide, jnp.bfloat16) for n in (6, 6, 5, 5, 0, 0)]
         + [pltpu.SMEM((SLOTS, ROWS), jnp.int32)] * 2
@@ -353,6 +355,13 @@
         + [pltpu.SemaphoreType.DMA((6,)), pltpu.SemaphoreType.DMA((48,)), pltpu.SemaphoreType.DMA((48,))],
         compiler_params=pltpu.CompilerParams(collective_id=0, has_side_effects=True, vmem_limit_bytes=48 * 1024 * 1024),
     )(*(pltpu.with_memory_space_constraint(x, pltpu.HBM) for x in (z_columns.T, p_columns.T, z_factor.reshape(tiles), d_density.reshape(tiles))))
+    out_x, out_f = pl.pallas_call(
+        deliver,
+        out_shape=[pltpu.HBM(tiles, f32)] * 2,
+        in_specs=[pl.BlockSpec(memory_space=pltpu.VMEM)] * 2,
+        out_specs=[pl.BlockSpec(memory_space=pltpu.HBM)] * 2,
+        scratch_shapes=[pltpu.SemaphoreType.DMA((2,))],
+    )(*(pltpu.with_memory_space_constraint(x, pltpu.VMEM) for x in (out_x, out_f)))
     shape = z_factor.shape
     return out_x.reshape(shape), out_f.reshape(shape)
 

time: 63.1 us -> 62.4 us (0.989)
  local copies, waits for them, and re-layouts: 1.94 us -> 0 us
  Pallas kernels: 60.4 us -> 61.6 us
    unnamed x2 -> x0, local copies, waits for them, and re-layouts: 1.94 us -> none
    pallas_call x1 -> x2, Pallas kernels: 60.4 us -> 61.6 us  [the longest x1 60.3 us: shards(): pl.pallas_call(kernel, out_shape=[pltpu.VMEM(tiles, f32)] * 2, in_specs=[...]
where the time goes in v4:
time: 62.4 us; the launch traced here: 62.3 us
  Pallas kernels  61.6 us (99%)
  between operations  0.64 us (1%)
    pallas_call x1, Pallas kernels, shards(): pl.pallas_call(kernel, out_shape=[pltpu.VMEM(tiles, f32)] * 2, in_specs=[...  60.3 us
    pallas_call x1, Pallas kernels, shards(): pl.pallas_call(deliver, out_shape=[pltpu.HBM(tiles, f32)] * 2, in_specs=[...  1.33 us

profile of v4, /device:TPU:1, one launch (start us, length us, event | category | flops | bytes accessed | tf_op | source)
XLA Modules:
  0.0 62.3 jit_solution(2559080954707092399)
XLA Ops:
  0.6 60.3 %shard_map.59 = (f32[16,128,128]{2,1,0:T(8,128)S(1)}, f32[16,128,128]{2,1,0:T(8,128)S(1)}) custom-call(s32[8,512]{1,0:T(8,128)} %bitcast.8, s32[8,512]{1,0:T(8,128)} %bitcast.9, f32[16,128,128]{2,1,0:T(8,128)} %bitcast.6, f32[16,128,128]{2,1,0:T(8,128)} %bitcast.7), custom_call_target="tpu_custom_call" | custom-call | tf_op jit(solution)/shard_map/pallas_call | solution.py:345
  60.9 1.3 %shard_map.60 = (f32[16,128,128]{2,1,0:T(8,128)}, f32[16,128,128]{2,1,0:T(8,128)}) custom-call(f32[16,128,128]{2,1,0:T(8,128)S(1)} %get-tuple-element.6.x, f32[16,128,128]{2,1,0:T(8,128)S(1)} %get-tuple-element.7.f), custom_call_target="tpu_custom_call" | custom-call | tf_op jit(solution)/shard_map/pallas_call | solution.py:358

commit v5 on v4

--- a/solution.py
+++ b/solution.py
@@ -237,18 +237,18 @@
     offer(2)
     send("p2")
 
-    @pl.loop(0, 5)
-    def _(q):
-        rd[q] = product(own_z(OWN), yd[q], TN)
-
-    send("r1")
     relay("via2", CUT_V, "zx2")
-    send("r2")
     arrive(*all_of("zx1", CUT_V))
     gather_y(1)
     arrive("p1", "p2")
     pd[0] += pr[0] + pr[1]
     send("s")
+
+    @pl.loop(0, 5)
+    def _(q):
+        rd[q] = product(own_z(OWN), yd[q], TN)
+
+    send("r1", "r2")
     arrive("zx0")
     gather_y(0)
     arrive(*all_of("zx2", CUT_V))

time: 62.4 us -> 62.3 us (level)
  no operation moved by 1% of the time
where the time goes in v5:
time: 62.3 us; the launch traced here: 62.1 us
  Pallas kernels  61.5 us (99%)
  between operations  0.64 us (1%)
    pallas_call x1, Pallas kernels, shards(): pl.pallas_call(kernel, out_shape=[pltpu.VMEM(tiles, f32)] * 2, in_specs=[...  60.2 us
    pallas_call x1, Pallas kernels, shards(): pl.pallas_call(deliver, out_shape=[pltpu.HBM(tiles, f32)] * 2, in_specs=[...  1.33 us

profile of v5, /device:TPU:1, one launch (start us, length us, event | category | flops | bytes accessed | tf_op | source)
XLA Modules:
  0.0 62.1 jit_solution(433888224395411795)
XLA Ops:
  0.6 60.2 %shard_map.59 = (f32[16,128,128]{2,1,0:T(8,128)S(1)}, f32[16,128,128]{2,1,0:T(8,128)S(1)}) custom-call(s32[8,512]{1,0:T(8,128)} %bitcast.8, s32[8,512]{1,0:T(8,128)} %bitcast.9, f32[16,128,128]{2,1,0:T(8,128)} %bitcast.6, f32[16,128,128]{2,1,0:T(8,128)} %bitcast.7), custom_call_target="tpu_custom_call" | custom-call | tf_op jit(solution)/shard_map/pallas_call | solution.py:345
  60.8 1.3 %shard_map.60 = (f32[16,128,128]{2,1,0:T(8,128)}, f32[16,128,128]{2,1,0:T(8,128)}) custom-call(f32[16,128,128]{2,1,0:T(8,128)S(1)} %get-tuple-element.6.x, f32[16,128,128]{2,1,0:T(8,128)S(1)} %get-tuple-element.7.f), custom_call_target="tpu_custom_call" | custom-call | tf_op jit(solution)/shard_map/pallas_call | solution.py:358
